TPU v7x, 32 devices: a whole 2x2x4 slice. The times are simulated.
32 devices in a mesh: batch: 4 (over z), pos: 8 (over y, x, core).
Axes of the slice: x: 2, y: 2, z: 4, core: 2. Of those that a mesh axis runs over, the one named last changes fastest.
Arguments:
- inputs: bfloat16 [4, 4096, 1536], P('batch', 'pos'), may hold values from -6 to 6
- bn_scale: float32 [1536], replicated, may hold values from 0.25 to 1.75
- bn_shift: float32 [1536], replicated, may hold values from -2 to 2
- mid_scale: float32 [384], replicated, may hold values from 0.25 to 1.75
- mid_shift: float32 [384], replicated, may hold values from -2 to 2
- dilated_weight: bfloat16 [1536, 3, 384], P('batch'), may hold values from -0.09375 to 0.09375
- w_point: bfloat16 [384, 1536], P('batch'), may hold values from -0.3125 to 0.3125
- head: bfloat16 [5120, 1536], P('pos'), may hold values from -0.15625 to 0.15625
- targets: bfloat16 [4, 4096, 512], P('batch', 'pos'), may hold values from 0 to 2
- assay_slots: int32 [4, 512], P('batch', 'pos'), may hold values from 0 to 639, as said below
- assay_counts: int32 [4, 8], P('batch', 'pos'), may hold values from 1 to 64, as said below
Outputs:
- d_inputs: bfloat16 [4, 4096, 1536], P('batch', 'pos')
- new_head: bfloat16 [5120, 1536], P('pos')
Inputs may be any that keep to these rules, and one draw needn't show every extreme that they name: `assay_slots`: within each block of 64 slots (one shard of one sequence) the entries are distinct. `assay_counts`: in every sequence some shard has all 64 slots live.
All inputs are finite; a program needn't handle non-finite values.
Results may differ from a plain program's by a relative error of at most 0.012.
Values may be sent and summed in bfloat16 or wider, within the bound.
A program may use at most 64 MiB of HBM per device.

v0:
```python
import jax
import jax.numpy as jnp
from jax import lax
from jax.sharding import PartitionSpec as P

DILATION_STEP = 32


def with_halo(shard, sides, width):
    for axis, dim in sides:
        peers, length = (lax.axis_size(axis), shard.shape[dim])
        up = [(i, (i + 1) % peers) for i in range(peers - 1)]
        down = [(j, i) for i, j in up]
        last = lax.slice_in_dim(shard, length - width, length, axis=dim)
        initial = lax.slice_in_dim(shard, 0, width, axis=dim)
        before = lax.ppermute(last, axis, up)
        after = lax.ppermute(initial, axis, down)
        shard = jnp.concatenate([before, shard, after], axis=dim)
    return shard


def gelu_slope(value):
    return jax.jvp(jax.nn.gelu, (value,), (jnp.ones_like(value),))[1]


def per_device(
    inputs,
    bn_scale,
    bn_shift,
    mid_scale,
    mid_shift,
    dilated_weight,
    w_point,
    head,
    targets,
    assay_slots,
    assay_counts,
):
    contract = (((1,), (1,)), ((), ()))
    kernel, pointwise = (
        lax.all_gather(dilated_weight, "batch", axis=0, tiled=True),
        lax.all_gather(w_point, "batch", axis=0, tiled=True),
    )
    stream = inputs[0]
    rows = stream.shape[0]
    window_length = DILATION_STEP
    first = stream.astype(jnp.float32) * bn_scale + bn_shift
    acted = jax.nn.gelu(first).astype(jnp.bfloat16)
    padded_input = with_halo(acted, (("pos", 0),), window_length)
    hidden_state = jnp.dot(
        padded_input[0:rows], kernel[:, 0, :], preferred_element_type=jnp.float32
    )
    hidden_state = hidden_state + jnp.dot(
        padded_input[window_length : window_length + rows],
        kernel[:, 1, :],
        preferred_element_type=jnp.float32,
    )
    hidden_state = hidden_state + jnp.dot(
        padded_input[2 * window_length : 2 * window_length + rows],
        kernel[:, 2, :],
        preferred_element_type=jnp.float32,
    )
    second = hidden_state * mid_scale + mid_shift
    mid = jax.nn.gelu(second).astype(jnp.bfloat16)
    embed = (
        stream.astype(jnp.float32) + jnp.dot(mid, pointwise, preferred_element_type=jnp.float32)
    ).astype(jnp.bfloat16)
    slots = assay_slots[0]
    slot_count = slots.shape[0]
    chosen = head[slots]
    live_mark = (jnp.arange(slot_count) < assay_counts[0, 0]).astype(jnp.bfloat16)
    selected, live_all = (
        lax.all_gather(chosen, "pos", axis=0, tiled=True),
        lax.all_gather(live_mark, "pos", axis=0, tiled=True),
    )
    pre = lax.dot_general(embed, selected, contract, preferred_element_type=jnp.float32)
    goal = targets[0].astype(jnp.float32)
    delta = (
        live_all.astype(jnp.float32) * (jax.nn.softplus(pre) - goal) * jax.nn.sigmoid(pre)
    ).astype(jnp.bfloat16)
    back = jnp.dot(delta, selected, preferred_element_type=jnp.float32).astype(jnp.bfloat16)
    dmid = lax.dot_general(back, pointwise, contract, preferred_element_type=jnp.float32)
    dhid = (dmid * gelu_slope(second) * mid_scale).astype(jnp.bfloat16)
    padded_grad = with_halo(dhid, (("pos", 0),), window_length)
    dact = lax.dot_general(
        padded_grad[2 * window_length : 2 * window_length + rows],
        kernel[:, 0, :],
        contract,
        preferred_element_type=jnp.float32,
    )
    dact = dact + lax.dot_general(
        padded_grad[window_length : window_length + rows],
        kernel[:, 1, :],
        contract,
        preferred_element_type=jnp.float32,
    )
    dact = dact + lax.dot_general(
        padded_grad[0:rows], kernel[:, 2, :], contract, preferred_element_type=jnp.float32
    )
    d_inputs = (back.astype(jnp.float32) + dact * gelu_slope(first) * bn_scale).astype(jnp.bfloat16)
    owned = lax.psum_scatter(
        lax.dot_general(
            delta, embed, (((0,), (0,)), ((), ())), preferred_element_type=jnp.float32
        ).astype(jnp.bfloat16),
        "pos",
        scatter_dimension=0,
        tiled=True,
    ).astype(jnp.float32)
    spread = jnp.zeros((head.shape[0], owned.shape[1]), jnp.float32).at[slots].add(owned)
    d_head = lax.psum(spread.astype(jnp.bfloat16), "batch").astype(jnp.float32)
    new_head = (head.astype(jnp.float32) - 0.004 * d_head).astype(jnp.bfloat16)
    return (d_inputs[None], new_head)


def solution(mesh):
    in_specs = (
        P("batch", "pos", None),
        P(),
        P(),
        P(),
        P(),
        P("batch", None, None),
        P("batch", None),
        P("pos", None),
        P("batch", "pos", None),
        P("batch", "pos"),
        P("batch", "pos"),
    )
    out_specs = (P("batch", "pos", None), P("pos", None))
    return jax.shard_map(
        per_device, mesh=mesh, in_specs=in_specs, out_specs=out_specs, check_vma=False
    )
```

profile of v0, /device:TPU:0, one launch (start us, length us, event | category | flops | bytes accessed | tf_op | source)
XLA Modules:
  0.0 286.1 jit_solution(2264082619135657359)
XLA Ops:
  7.2 0.0 copy-start.11
  7.2 0.0 all-gather.5.cloned.1.call-start
  7.3 0.7 all-gather.5.cloned.1.call-update
  7.9 0.0 all-gather.7.cloned.1.call-start
  8.0 0.7 all-gather.7.cloned.1.call-update
  8.7 0.0 all-gather.9.cloned.1.call-start
  8.7 0.7 fusion.71
  9.4 3.4 %gather_fusion = bf16[64,1536]{1,0:T(8,128)(2,1)} fusion(bf16[640,1536]{1,0:T(8,128)(2,1)} %param.18, s32[1024]{0:T(1024)S(1)} %pad_clamp_fusion), kind=kCustom, calls=%fused_computation | custom fusion | bytes 393472 | tf_op jit(solution)/shard_map/gather | solution.py:70
  12.8 0.0 all-gather.9.cloned.1.call-update
  12.8 0.0 reduce-scatter.2.cloned.1.call-start
  12.9 1.3 fusion.12
  14.2 2.4 collective-permute-start
  16.6 1.3 collective-permute-start.1
  18.5 0.6 dynamic-slice
  19.7 0.2 dynamic-update-slice
  19.9 17.5 %all-reduce = bf16[512]{0:T(512)(128)(2,1)S(1)} all-reduce(bf16[512]{0:T(512)(128)(2,1)S(1)} %dynamic-update-slice), channel_id=1, replica_groups=mesh['batch'=4,'pos'=8] {'pos'}, use_global_device_ids=true, to_apply=%add | all-reduce | flops 512 | bytes 2048
  37.4 44.9 %all-gather.5.cloned.1.call-done = bf16[1536,3,384]{2,0,1:T(8,128)(2,1)} async-done(((bf16[384,3,384]{2,0,1:T(8,128)(2,1)}), bf16[1536,3,384]{2,0,1:T(8,128)(2,1)}) %all-gather.5.cloned.1.call-update) | async-done | bytes 3538960 | tf_op jit(solution)/shard_map/all_gather | solution.py:41
  82.3 2.8 fusion.38
  85.2 0.0 copy-start.10
  85.2 0.0 collective-permute-done.1
  85.2 1.9 fusion.34
  87.1 0.0 collective-permute-done
  87.1 1.9 fusion.44
  89.0 23.9 %all-gather.7.cloned.1.call-done = bf16[384,1536]{1,0:T(8,128)(2,1)} async-done(((bf16[96,1536]{1,0:T(8,128)(2,1)}), bf16[384,1536]{1,0:T(8,128)(2,1)}) %all-gather.7.cloned.1.call-update) | async-done | bytes 1179664 | tf_op jit(solution)/shard_map/all_gather | solution.py:42
  113.0 2.5 fusion.29
  115.5 0.0 copy-start.12
  115.5 24.8 %all-gather.9.cloned.1.call-done = bf16[512,1536]{1,0:T(8,128)(2,1)} async-done(((bf16[64,1536]{1,0:T(8,128)(2,1)}), bf16[512,1536]{1,0:T(8,128)(2,1)}) %all-gather.9.cloned.1.call-update) | async-done | bytes 1572880 | tf_op jit(solution)/shard_map/all_gather | solution.py:73
  140.3 2.5 fusion.90
  142.8 1.0 copy-done.13
  143.7 4.3 %convolution_convert_fusion = bf16[512,1536]{1,0:T(8,128)(2,1)} fusion(bf16[512,1536]{1,0:T(8,128)(2,1)} %copy-done.12, f32[512,512]{1,0:T(8,128)S(1)} %fusion.90, bf16[1,512,512]{2,1,0:T(8,128)(2,1)S(1)} %copy-done.8, f32[512]{0:T(512)S(1)} %convert_element_type.70), kind=kOutput, calls=%fused_computation.39 | convolution fusion | flops 809762816 | bytes 4720640 | tf_op jit(solution)/shard_map/dot_general | solution.py:102
  148.1 0.0 reduce-scatter.2.cloned.1.call-update
  148.1 0.0 all-reduce.3.cloned.1.call-start
  148.2 4.1 %convolution_convert_fusion.1 = bf16[512,1536]{1,0:T(8,128)(2,1)} fusion(bf16[512,1536]{1,0:T(8,128)(2,1)S(1)} %copy-done.6, f32[512,512]{1,0:T(8,128)} %copy-done.13, bf16[1,512,512]{2,1,0:T(8,128)(2,1)} %param.19, f32[512]{0:T(512)S(1)} %convert_element_type.70), kind=kOutput, calls=%fused_computation.40 | convolution fusion | flops 809762816 | bytes 4720640 | tf_op jit(solution)/shard_map/dot_general | solution.py:81
  152.2 34.5 %reduce-scatter.2.cloned.1.call-done = bf16[64,1536]{1,0:T(8,128)(2,1)} async-done(((bf16[512,1536]{1,0:T(8,128)(2,1)}), bf16[64,1536]{1,0:T(8,128)(2,1)}) %reduce-scatter.2.cloned.1.call-update) | async-done | bytes 196624 | tf_op jit(solution)/shard_map/reduce_scatter | solution.py:101
  186.7 3.7 %scatter_custom_fusion = f32[640,1536]{1,0:T(8,128)} fusion(s32[64]{0:T(128)S(1)} %fusion.71, f32[]{:T(128)} %constant.15.clone.1, bf16[64,1536]{1,0:T(8,128)(2,1)} %reduce-scatter.2.cloned.1.call-done), kind=kCustom, calls=%fused_computation.43 | custom fusion | flops 196608 | bytes 4128772 | tf_op jit(solution)/shard_map/scatter-add | solution.py:109
  190.4 3.7 %convert_element_type.89 = bf16[640,1536]{1,0:T(8,128)(2,1)} convert(f32[640,1536]{1,0:T(8,128)} %scatter_custom_fusion) | non-fusion elementwise | flops 983040 | bytes 5898240 | tf_op jit(solution)/shard_map/convert_element_type | solution.py:110
  194.1 0.0 all-reduce.3.cloned.1.call-update
  194.1 3.0 %fusion.45 = bf16[512,384]{1,0:T(8,128)(2,1)S(1)} fusion(bf16[512,1536]{1,0:T(8,128)(2,1)} %convolution_convert_fusion.1, bf16[384,1536]{1,0:T(8,128)(2,1)S(1)} %copy-done.7, f32[512,384]{1,0:T(8,128)} %fusion.44, f32[384]{0:T(512)S(1)} %copy-done.10), kind=kOutput, calls=%fused_computation.59 | convolution fusion | flops 607715328 | bytes 3933696 | tf_op jit(solution)/shard_map/dot_general | solution.py:82
  197.2 1.3 collective-permute-start.2
  198.5 3.0 %collective-permute-start.3 = (bf16[32,384]{1,0:T(8,128)(2,1)S(1)}, bf16[32,384]{1,0:T(8,128)(2,1)S(1)}, u32[]{:S(2)}, u32[]{:S(2)}) collective-permute-start(bf16[32,384]{1,0:T(8,128)(2,1)S(1)} %get-tuple-element.5), channel_id=1, source_target_pairs={{0,1},{1,2},{2,3},{3,4},{4,5},{5,6},{6,7},{8,9},{9,10},{10,11},{11... | collective-permute-start | bytes 73736 | tf_op jit(solution)/shard_map/ppermute | solution.py:16
  201.5 1.0 fusion.50
  202.5 0.0 copy-start.14
  202.6 1.0 fusion.51
  203.6 0.0 copy-start
  203.6 0.3 copy-done.14
  204.0 4.0 %fusion.30 = bf16[1,512,1536]{2,1,0:T(8,128)(2,1)} fusion(bf16[1,512,1536]{2,1,0:T(8,128)(2,1)S(1)} %copy-done.1, f32[512,1536]{1,0:T(8,128)S(1)} %fusion.51, f32[512,1536]{1,0:T(8,128)S(1)} %fusion.50, bf16[512,1536]{1,0:T(8,128)(2,1)S(1)} %copy-done.14, f32[1536]{0:T(1024)S(1)} %copy-done.4, f32[1536]{0:T(1024)S(1)} %copy-done.5, ...), kind=kOutput, calls=%fused_computation.42 | convolution fusion | flops 625213440 | bytes 12623872 | tf_op jit(solution)/shard_map/dot_general | solution.py:85
  207.9 68.3 %all-reduce.3.cloned.1.call-done = bf16[640,1536]{1,0:T(8,128)(2,1)} async-done(((bf16[640,1536]{1,0:T(8,128)(2,1)}), bf16[640,1536]{1,0:T(8,128)(2,1)}) %all-reduce.3.cloned.1.call-update) | async-done | bytes 1966096 | tf_op jit(solution)/shard_map/psum | solution.py:110
  276.2 3.4 %subtract_convert_fusion = bf16[640,1536]{1,0:T(8,128)(2,1)} fusion(bf16[640,1536]{1,0:T(8,128)(2,1)} %all-reduce.3.cloned.1.call-done, bf16[640,1536]{1,0:T(8,128)(2,1)S(1)} %copy-done), kind=kLoop, calls=%fused_computation.9 | loop fusion | flops 4915200 | bytes 5898240 | tf_op jit(solution)/shard_map/convert_element_type | solution.py:111
  (31 shorter events, 0.1 us)
Async XLA Ops:
  7.2 11.4 %copy-start.11 = (u32[32]{0:T(128)S(1)}, u32[32]{0:T(128)}, u32[]{:S(2)}) copy-start(u32[32]{0:T(128)} %constant.34) | copy-start | bytes 388
  7.2 5.7 %copy-start.1 = (bf16[1,512,1536]{2,1,0:T(8,128)(2,1)S(1)}, bf16[1,512,1536]{2,1,0:T(8,128)(2,1)}, u32[]{:S(2)}) copy-start(bf16[1,512,1536]{2,1,0:T(8,128)(2,1)} %param.11) | copy-start | bytes 4718596
  7.2 5.7 %copy-start.4 = (f32[1536]{0:T(1024)S(1)}, f32[1536]{0:T(1024)}, u32[]{:S(2)}) copy-start(f32[1536]{0:T(1024)} %param.13) | copy-start | bytes 18436
  7.2 5.7 %copy-start.5 = (f32[1536]{0:T(1024)S(1)}, f32[1536]{0:T(1024)}, u32[]{:S(2)}) copy-start(f32[1536]{0:T(1024)} %param.12) | copy-start | bytes 18436
  7.2 75.1 %all-gather.5.cloned.1.call-start = ((), (), s32[]{:S(2)}) async-start(), calls=%async_computation.1 | async-start | bytes 4423680 | tf_op jit(solution)/shard_map/all_gather | solution.py:41
  7.9 105.0 %all-gather.7.cloned.1.call-start = ((), (), s32[]{:S(2)}) async-start(), calls=%async_computation.2 | async-start | bytes 1474560 | tf_op jit(solution)/shard_map/all_gather | solution.py:42
  8.7 131.6 %all-gather.9.cloned.1.call-start = ((), (), s32[]{:S(2)}) async-start(), calls=%async_computation.5 | async-start | bytes 1769472 | tf_op jit(solution)/shard_map/all_gather | solution.py:73
  12.8 173.9 %reduce-scatter.2.cloned.1.call-start = ((), (), s32[]{:S(2)}) async-start(), calls=%async_computation.3 | async-start | bytes 1769472 | tf_op jit(solution)/shard_map/reduce_scatter | solution.py:101
  14.2 72.9 %collective-permute-start = (bf16[32,1536]{1,0:T(8,128)(2,1)S(1)}, bf16[32,1536]{1,0:T(8,128)(2,1)S(1)}, u32[]{:S(2)}, u32[]{:S(2)}) collective-permute-start(bf16[32,1536]{1,0:T(8,128)(2,1)S(1)} %get-tuple-element.2), channel_id=1, source_target_pairs={{0,1},{1,2},{2,3},{3,4},{4,5},{5,6},{6,7},{8,9},{9,10},{10,11},{11... | collective-permute-start | bytes 294920 | tf_op jit(solution)/shard_map/ppermute | solution.py:16
  16.6 68.6 %collective-permute-start.1 = (bf16[32,1536]{1,0:T(8,128)(2,1)S(1)}, bf16[32,1536]{1,0:T(8,128)(2,1)}, u32[]{:S(2)}, u32[]{:S(2)}) collective-permute-start(bf16[32,1536]{1,0:T(8,128)(2,1)S(1)} %get-tuple-element.3), channel_id=1, source_target_pairs={{1,0},{2,1},{3,2},{4,3},{5,4},{6,5},{7,6},{9,8},{10,9},{11,10},{12... | collective-permute-start | bytes 294920 | tf_op jit(solution)/shard_map/ppermute | solution.py:17
  82.3 2.9 %copy-start.2 = (bf16[1536,3,384]{2,0,1:T(8,128)(2,1)S(1)}, bf16[1536,3,384]{2,0,1:T(8,128)(2,1)}, u32[]{:S(2)}) copy-start(bf16[1536,3,384]{2,0,1:T(8,128)(2,1)} %all-gather.5.cloned.1.call-done) | copy-start | bytes 10616836
  85.1 1.9 copy-start.9
  85.2 1.9 copy-start.10
  115.5 24.8 %copy-start.12 = (bf16[512,1536]{1,0:T(8,128)(2,1)}, bf16[512,1536]{1,0:T(8,128)(2,1)S(1)}, u32[]{:S(2)}) copy-start(bf16[512,1536]{1,0:T(8,128)(2,1)S(1)} %fusion.29) | copy-start | bytes 4718596
  140.3 3.5 %copy-start.8 = (bf16[1,512,512]{2,1,0:T(8,128)(2,1)S(1)}, bf16[1,512,512]{2,1,0:T(8,128)(2,1)}, u32[]{:S(2)}) copy-start(bf16[1,512,512]{2,1,0:T(8,128)(2,1)} %param.19) | copy-start | bytes 1572868
  142.8 1.0 copy-start.13
  143.7 4.4 %copy-start.6 = (bf16[512,1536]{1,0:T(8,128)(2,1)S(1)}, bf16[512,1536]{1,0:T(8,128)(2,1)}, u32[]{:S(2)}) copy-start(bf16[512,1536]{1,0:T(8,128)(2,1)} %all-gather.9.cloned.1.call-done) | copy-start | bytes 4718596
  148.1 128.1 %all-reduce.3.cloned.1.call-start = ((), (), s32[]{:S(2)}) async-start(), calls=%async_computation.4 | async-start | bytes 3932160 | tf_op jit(solution)/shard_map/psum | solution.py:110
  190.4 3.7 %copy-start.7 = (bf16[384,1536]{1,0:T(8,128)(2,1)S(1)}, bf16[384,1536]{1,0:T(8,128)(2,1)}, u32[]{:S(2)}) copy-start(bf16[384,1536]{1,0:T(8,128)(2,1)} %all-gather.7.cloned.1.call-done) | copy-start | bytes 3538948
  194.1 7.4 %copy-start.3 = (bf16[1536,3,384]{2,0,1:T(8,128)(2,1)S(1)}, bf16[1536,3,384]{2,0,1:T(8,128)(2,1)}, u32[]{:S(2)}) copy-start(bf16[1536,3,384]{2,0,1:T(8,128)(2,1)} %all-gather.5.cloned.1.call-done) | copy-start | bytes 10616836
  197.2 6.4 %collective-permute-start.2 = (bf16[32,384]{1,0:T(8,128)(2,1)S(1)}, bf16[32,384]{1,0:T(8,128)(2,1)S(1)}, u32[]{:S(2)}, u32[]{:S(2)}) collective-permute-start(bf16[32,384]{1,0:T(8,128)(2,1)S(1)} %get-tuple-element.4), channel_id=1, source_target_pairs={{1,0},{2,1},{3,2},{4,3},{5,4},{6,5},{7,6},{9,8},{10,9},{11,10},{12... | collective-permute-start | bytes 73736 | tf_op jit(solution)/shard_map/ppermute | solution.py:17
  198.5 4.1 %collective-permute-start.3 = (bf16[32,384]{1,0:T(8,128)(2,1)S(1)}, bf16[32,384]{1,0:T(8,128)(2,1)S(1)}, u32[]{:S(2)}, u32[]{:S(2)}) collective-permute-start(bf16[32,384]{1,0:T(8,128)(2,1)S(1)} %get-tuple-element.5), channel_id=1, source_target_pairs={{0,1},{1,2},{2,3},{3,4},{4,5},{5,6},{6,7},{8,9},{9,10},{10,11},{11... | collective-permute-start | bytes 73736 | tf_op jit(solution)/shard_map/ppermute | solution.py:16
  202.5 1.4 copy-start.14
  203.6 72.6 %copy-start = (bf16[640,1536]{1,0:T(8,128)(2,1)S(1)}, bf16[640,1536]{1,0:T(8,128)(2,1)}, u32[]{:S(2)}) copy-start(bf16[640,1536]{1,0:T(8,128)(2,1)} %param.18) | copy-start | bytes 5898244
Sparse Core Ops, SparseCore 0:
  9.6 72.6 all-gather.4
  83.9 29.0 all-gather.6
  115.4 24.7 all-gather.8
  148.2 38.4 reduce-scatter.1
  194.2 81.9 all-reduce.2
where the time goes:
time: 287 us; the launch traced here: 286 us
  waiting for transfers between devices  198 us (69%)
  matrix products  29 us (10%)
  blocking collectives  17.5 us (6%)
  between operations  15.3 us (5%)
  other arithmetic  12.7 us (4%)
  starting transfers between devices  8.18 us (3%)
  local copies, waits for them, and re-layouts  5.62 us (2%)
    psum x1, waiting for transfers between devices, per_device(): d_head = lax.psum(spread.astype(jnp.bfloat16), 'batch').astype(jnp.float32)  68.3 us
    all_gather x1, waiting for transfers between devices, per_device(): lax.all_gather(dilated_weight, 'batch', axis=0, tiled=True)  44.9 us
    reduce_scatter x1, waiting for transfers between devices, per_device(): lax.psum_scatter(lax.dot_general(delta, embed, (((0,), (0,)), ((), ())),...  34.5 us
    all_gather x1, waiting for transfers between devices, per_device(): lax.all_gather(chosen, 'pos', axis=0, tiled=True)  24.8 us
    all_gather x1, waiting for transfers between devices, per_device(): lax.all_gather(w_point, 'batch', axis=0, tiled=True)  23.9 us
    unnamed x1, blocking collectives  17.5 us
  transfers between devices with their start and end apart: 9, of which 5 were waited for; matrix products, arithmetic and copies ran while one was open for 10% of the time, Pallas kernels for 0%

commit v1 on v0

v1 whole, which is shorter than its diff:
```python
import functools

import jax
import jax.numpy as jnp
from jax import lax
from jax.experimental import pallas as pl
from jax.experimental.pallas import tpu as pltpu
from jax.sharding import PartitionSpec as P

STEP = 32
MESH = pl.DeviceIdType.MESH
F32 = jnp.float32
BF16 = jnp.bfloat16
ROOT = 0.7978845608028654
CUBE = 0.044715


def gelu(v):
    return 0.5 * v * (1.0 + jnp.tanh(ROOT * (v + CUBE * v * v * v)))


def gelu_slope(v):
    sq = v * v
    t = jnp.tanh(ROOT * (v + CUBE * v * sq))
    return 0.5 * (1.0 + t) + 0.5 * v * (1.0 - t * t) * (ROOT * (1.0 + 3.0 * CUBE * sq))


def dot(a, b):
    return jnp.dot(a, b, preferred_element_type=F32)


def dot_t(a, b):
    return lax.dot_general(a, b, (((1,), (1,)), ((), ())), preferred_element_type=F32)


def tdot(a, b):
    return lax.dot_general(a, b, (((0,), (0,)), ((), ())), preferred_element_type=F32)


def kernel(nb, npos, spread, *refs):
    refs = list(refs)
    take = lambda n: [refs.pop(0) for _ in range(n)]
    x, bsc, bsh, msc, msh, packed = take(6)
    if not spread:
        (wp,) = take(1)
    head, goal, meta = take(3)
    d_in, new_head = take(2)
    if spread:
        w, wp = take(2)
    else:
        w = packed
    acted, hidden, mid, embed, sel, delta, back, dpad, xh = take(9)
    grads, r1buf, part, r2buf, rows_all, meta_all, onehot = take(7)
    (halo_s, halo_r, meta_s, meta_r, sel_s, sel_r, self_s, self_r, r1_s, r1_r, r2_s, r2_r, r3_s, r3_r) = take(14)
    if spread:
        own_sem, w1_s, w1_r, w2_s, w2_r, wf_s, wf_r = take(7)

    z = lax.axis_index("batch")
    p = lax.axis_index("pos")
    chip, core = p // 2, p % 2
    nchip = npos // 2
    sib = chip * 2 + (1 - core)
    nrows, width = x.shape
    nz = w.shape[0]
    cw = width // nz
    hid = mid.shape[1]
    nslot = delta.shape[1]
    aslot = sel.shape[1]

    def rc(src, dst, s, r, zz, pp):
        return pltpu.make_async_remote_copy(
            src_ref=src, dst_ref=dst, send_sem=s, recv_sem=r, device_id=(zz, pp), device_id_type=MESH
        )

    def at_chip(d):
        return lax.rem(chip + d, nchip)

    def from_chip(d):
        return lax.rem(chip - d + nchip, nchip)

    bar = pltpu.get_barrier_semaphore()
    for d in range(1, npos):
        pl.semaphore_signal(bar, inc=1, device_id=(z, lax.rem(p + d, npos)), device_id_type=MESH)
    for d in range(1, nb):
        pl.semaphore_signal(bar, inc=1, device_id=(lax.rem(z + d, nb), p), device_id_type=MESH)
    pl.semaphore_wait(bar, npos - 1 + nb - 1)

    sends = []

    def go(c):
        c.start()
        sends.append(c)

    right, left = lax.rem(p + 1, npos), lax.rem(p + npos - 1, npos)

    def chain(src, dst, ss, rr):
        def copy(di, k, first):
            zz = z - k if di == 0 else z + k
            to = z + 1 if di == 0 else z - 1
            return rc(src if first else dst(zz), dst(zz), ss.at[di, k], rr.at[di, k], to, p)

        def can_send(di, k):
            if di == 0:
                return jnp.logical_and(z + 1 < nb, z - k >= 0)
            return jnp.logical_and(z - 1 >= 0, z + k < nb)

        def start(di, k):
            @pl.when(can_send(di, k))
            def _():
                copy(di, k, k == 0).start()

        def arrive(di, k, body):
            has = (z - k - 1 >= 0) if di == 0 else (z + k + 1 < nb)

            @pl.when(has)
            def _():
                zz = z - k - 1 if di == 0 else z + k + 1
                rc(dst(zz), dst(zz), ss.at[di, k], rr.at[di, k], z, sib).wait_recv()

            if k + 1 < nb - 1:
                start(di, k + 1)
            if body is not None:
                @pl.when(has)
                def _():
                    body(z - k - 1 if di == 0 else z + k + 1)

        def finish():
            for di in (0, 1):
                for k in range(nb - 1):
                    @pl.when(can_send(di, k))
                    def _():
                        copy(di, k, k == 0).wait_send()

        return start, arrive, finish

    if spread:
        w_start, w_arrive, w_finish = chain(packed.at[p], lambda zz: w.at[zz, p], w1_s, w1_r)
        w_start(0, 0)
        w_start(1, 0)
    go(rc(x.at[pl.ds(0, STEP)], xh.at[1], halo_s.at[0], halo_r.at[1], z, left))
    go(rc(x.at[pl.ds(nrows - STEP, STEP)], xh.at[0], halo_s.at[1], halo_r.at[0], z, right))
    for d in range(1, nb):
        go(rc(meta, meta_all.at[z], meta_s.at[d], meta_r.at[d], lax.rem(z + d, nb), p))
    if spread:
        own = pltpu.make_async_copy(packed, w.at[z], own_sem)
        own.start()

    ntrk = head.shape[0]

    def marks(m):
        return (m[:, 0:1] == lax.broadcasted_iota(jnp.int32, (aslot, ntrk), 1)).astype(BF16)

    sel[p] = dot(marks(meta[...]), head[...]).astype(BF16)
    for d in range(1, nchip):
        go(rc(sel.at[p], sel.at[p], sel_s.at[d], sel_r.at[d], z, at_chip(d) * 2 + core))
    go(rc(sel.at[p], sel.at[p], self_s.at[0], self_r.at[0], z, sib))

    def act_chunk(i):
        cols = pl.ds(i * cw, cw)
        first = x[:, cols].astype(F32) * bsc[:, cols] + bsh[:, cols]
        acted[i, STEP : STEP + nrows] = gelu(first).astype(BF16)

    def w_spread(di, k):
        def body(zz):
            for d in range(1, nchip):
                rc(w.at[zz, p], w.at[zz, p], w2_s.at[di, k, d], w2_r.at[di, k, d], z, at_chip(d) * 2 + core).start()
            rc(w.at[zz, p], w.at[zz, p], wf_s.at[di, k, 0], wf_r.at[di, k, 0], z, sib).start()

        w_arrive(di, k, body)

    def w_shard(di, k):
        zz = z - k - 1 if di == 0 else z + k + 1
        has = (zz >= 0) if di == 0 else (zz < nb)
        return zz, has

    def w_forward(di, k):
        zz, has = w_shard(di, k)

        @pl.when(has)
        def _():
            for d in range(1, nchip):
                q = from_chip(d) * 2 + core
                rc(w.at[zz, q], w.at[zz, q], w2_s.at[di, k, d], w2_r.at[di, k, d], z, sib).wait_recv()
                rc(w.at[zz, q], w.at[zz, q], wf_s.at[di, k, d], wf_r.at[di, k, d], z, sib).start()

    def w_ready(di, k):
        zz, has = w_shard(di, k)

        @pl.when(has)
        def _():
            for d in range(nchip):
                q = from_chip(d) * 2 + 1 - core
                rc(w.at[zz, q], w.at[zz, q], wf_s.at[di, k, d], wf_r.at[di, k, d], z, sib).wait_recv()
            conv(zz)

    def w_done(di, k):
        zz, has = w_shard(di, k)

        @pl.when(has)
        def _():
            for d in range(1, nchip):
                rc(w.at[zz, p], w.at[zz, p], w2_s.at[di, k, d], w2_r.at[di, k, d], z, sib).wait_send()
            for d in range(nchip):
                rc(w.at[zz, p], w.at[zz, p], wf_s.at[di, k, d], wf_r.at[di, k, d], z, sib).wait_send()

    def wrows(zz, lo, n):
        return w[zz, :, :, lo : lo + n].reshape(cw, n)

    def conv(zz):
        total = hidden[...]
        for k in range(3):
            total = total + dot(acted[zz, k * STEP : k * STEP + nrows], wrows(zz, k * hid, hid))
        hidden[...] = total

    def sel_forward():
        for d in range(1, nchip):
            q = from_chip(d) * 2 + core
            rc(sel.at[q], sel.at[q], sel_s.at[d], sel_r.at[d], z, sib).wait_recv()
            go(rc(sel.at[q], sel.at[q], self_s.at[d], self_r.at[d], z, sib))

    steps = range(nb - 1) if spread else range(0)
    hidden[...] = jnp.zeros_like(hidden)
    for i in range(nz):
        act_chunk(i)
        if i == 0:
            for k in steps[:1]:
                w_spread(0, k)
                w_spread(1, k)
        if i == 1:
            sel_forward()
            for k in steps[1:2]:
                w_spread(0, k)
                w_spread(1, k)
    for side, edge in ((0, 0), (1, npos - 1)):
        rc(xh.at[side], xh.at[side], halo_s.at[side], halo_r.at[side], z, sib).wait_recv()
        keep = jnp.where(p == edge, 0.0, 1.0)
        for i in range(nz):
            cols = pl.ds(i * cw, cw)
            first = xh[side, :, cols].astype(F32) * bsc[:, cols] + bsh[:, cols]
            lo = 0 if side == 0 else STEP + nrows
            acted[i, lo : lo + STEP] = (gelu(first) * keep).astype(BF16)
    if spread:
        for k in steps[2:]:
            w_forward(0, k - 2)
            w_forward(1, k - 2)
            w_spread(0, k)
            w_spread(1, k)
        own.wait()
        conv(z)
        for k in steps[max(0, len(steps) - 2) :]:
            w_forward(0, k)
            w_forward(1, k)
        for k in steps:
            w_ready(0, k)
            w_ready(1, k)
        rest = width // hid
        per = npos // rest
        for zz in range(nb):
            for q in range(rest):
                blk = w[zz, q * per : (q + 1) * per, :, 3 * hid : 4 * hid].reshape(cw // rest, hid)
                wp[zz * (cw // rest) : (zz + 1) * (cw // rest), q * hid : (q + 1) * hid] = blk
    else:
        for i in range(nz):
            conv(i)

    second = hidden[...] * msc[...] + msh[...]
    mid[...] = gelu(second).astype(BF16)
    half = 512
    for n in range(0, width, half):
        embed[:, n : n + half] = (x[:, n : n + half].astype(F32) + dot(mid[...], wp[:, n : n + half])).astype(BF16)

    for d in range(nchip):
        q = from_chip(d) * 2 + 1 - core
        rc(sel.at[q], sel.at[q], self_s.at[d], self_r.at[d], z, sib).wait_recv()

    group = 256
    per_group = group // aslot
    for j in range(0, nslot, group):
        s = sel[j // aslot : j // aslot + per_group].reshape(group, width)
        pre = dot_t(embed[...], s)
        e = jnp.exp(-jnp.abs(pre))
        soft = jnp.maximum(pre, 0.0) + jnp.log1p(e)
        sig = jnp.where(pre >= 0.0, 1.0, e) / (1.0 + e)
        delta[:, j : j + group] = ((soft - goal[:, j : j + group].astype(F32)) * sig).astype(BF16)
        for n in range(0, width, half):
            g = tdot(delta[:, j : j + group], embed[:, n : n + half]).astype(BF16)
            grads[j // aslot : j // aslot + per_group, :, n : n + half] = g.reshape(per_group, aslot, half)

    order = list(range(1, nchip)) + [0]
    for d in order:
        go(rc(grads.at[at_chip(d) * 2 + 1 - core], r1buf.at[d], r1_s.at[d], r1_r.at[d], z, sib))

    for n in range(0, width, half):
        back[:, n : n + half] = dot(delta[...], sel[:, :, n : n + half].reshape(nslot, half)).astype(BF16)

    for d in order:
        rc(r1buf.at[d], r1buf.at[d], r1_s.at[d], r1_r.at[d], z, sib).wait_recv()
        part[d] = (grads[at_chip(d) * 2 + core].astype(F32) + r1buf[d].astype(F32)).astype(BF16)
        if d:
            go(rc(part.at[d], r2buf.at[d], r2_s.at[d], r2_r.at[d], z, at_chip(d) * 2 + core))

    dmid = dot_t(back[...], wp[...])
    second = hidden[...] * msc[...] + msh[...]
    dpad[STEP : STEP + nrows] = (dmid * gelu_slope(second) * msc[...]).astype(BF16)
    go(rc(dpad.at[pl.ds(STEP, STEP)], dpad.at[pl.ds(STEP + nrows, STEP)], halo_s.at[2], halo_r.at[3], z, left))
    go(rc(dpad.at[pl.ds(nrows, STEP)], dpad.at[pl.ds(0, STEP)], halo_s.at[3], halo_r.at[2], z, right))

    total = part[0].astype(F32)
    for d in range(1, nchip):
        rc(r2buf.at[d], r2buf.at[d], r2_s.at[d], r2_r.at[d], z, sib).wait_recv()
        total = total + r2buf[d].astype(F32)
    rows_all[z] = total.astype(BF16)
    g_start, g_arrive, g_finish = chain(rows_all.at[z], lambda zz: rows_all.at[zz], r3_s, r3_r)
    g_start(0, 0)
    g_start(1, 0)

    for side, edge, lo in ((0, 0, 0), (1, npos - 1, STEP + nrows)):
        rc(dpad.at[pl.ds(lo, STEP)], dpad.at[pl.ds(lo, STEP)], halo_s.at[2], halo_r.at[2 + side], z, sib).wait_recv()

        @pl.when(p == edge)
        def _():
            dpad[lo : lo + STEP] = jnp.zeros((STEP, hid), BF16)

    arrivals = list(range(nb - 1))
    for i in range(nz):
        cols = pl.ds(i * cw, cw)
        dact = dot_t(dpad[2 * STEP : 2 * STEP + nrows], wrows(i, 0, hid))
        dact = dact + dot_t(dpad[STEP : STEP + nrows], wrows(i, hid, hid))
        dact = dact + dot_t(dpad[0:nrows], wrows(i, 2 * hid, hid))
        first = x[:, cols].astype(F32) * bsc[:, cols] + bsh[:, cols]
        d_in[:, cols] = (back[:, cols].astype(F32) + dact * gelu_slope(first) * bsc[:, cols]).astype(BF16)
        if i < nz - 1 and arrivals:
            k = arrivals.pop(0)
            g_arrive(0, k, None)
            g_arrive(1, k, None)
    for k in arrivals:
        g_arrive(0, k, None)
        g_arrive(1, k, None)

    for d in range(1, nb):
        zz = lax.rem(z - d + nb, nb)
        rc(meta_all.at[zz], meta_all.at[zz], meta_s.at[d], meta_r.at[d], z, sib).wait_recv()
    meta_all[z] = meta[...]
    for zz in range(nb):
        onehot[zz * aslot : (zz + 1) * aslot] = marks(meta_all[zz])
    for n in range(0, width, half):
        d_head = tdot(onehot[...], rows_all[:, :, n : n + half].reshape(nb * aslot, half))
        new_head[:, n : n + half] = (head[:, n : n + half].astype(F32) - 0.004 * d_head).astype(BF16)

    for c in sends:
        c.wait_send()
    g_finish()
    if spread:
        w_finish()
        for k in steps:
            w_done(0, k)
            w_done(1, k)


def per_device(nb, npos, inputs, bn_scale, bn_shift, mid_scale, mid_shift, dilated_weight, w_point, head, targets, assay_slots, assay_counts):
    x = inputs[0]
    nrows, width = x.shape
    cw, _, hid = dilated_weight.shape
    aslot = assay_slots.shape[1]
    nslot = targets.shape[2]
    ntrk = head.shape[0]
    spread = cw % (16 * npos) == 0 and cw % 128 == 0 and npos % (width // hid) == 0
    flat = dilated_weight.reshape(cw, 3 * hid)
    slots = jnp.where(jnp.arange(aslot) < assay_counts[0, 0], assay_slots[0], -1)
    meta = jnp.broadcast_to(slots[:, None], (aslot, 128))
    if spread:
        rest = width // hid
        wide = jnp.swapaxes(w_point.reshape(w_point.shape[0], rest, hid), 0, 1).reshape(cw, hid)
        weights = [jnp.concatenate([flat, wide], axis=1).reshape(npos, cw // npos, 4 * hid)]
        nz = nb
        weight_scratch = [
            pltpu.VMEM((nb, npos, cw // npos, 4 * hid), BF16),
            pltpu.VMEM((hid, width), BF16),
        ]
    else:
        nz = 4
        weights = [
            lax.all_gather(flat, "batch", axis=0, tiled=True).reshape(nz, 1, width // nz, 3 * hid),
            lax.all_gather(w_point, "batch", axis=0, tiled=True),
        ]
        weight_scratch = []
    nchip = npos // 2
    dma = pltpu.SemaphoreType.DMA
    scratch = weight_scratch + [
        pltpu.VMEM((nz, nrows + 2 * STEP, width // nz), BF16),
        pltpu.VMEM((nrows, hid), F32),
        pltpu.VMEM((nrows, hid), BF16),
        pltpu.VMEM((nrows, width), BF16),
        pltpu.VMEM((npos, aslot, width), BF16),
        pltpu.VMEM((nrows, nslot), BF16),
        pltpu.VMEM((nrows, width), BF16),
        pltpu.VMEM((nrows + 2 * STEP, hid), BF16),
        pltpu.VMEM((2, STEP, width), BF16),
        pltpu.VMEM((npos, aslot, width), BF16),
        pltpu.VMEM((nchip, aslot, width), BF16),
        pltpu.VMEM((nchip, aslot, width), BF16),
        pltpu.VMEM((nchip, aslot, width), BF16),
        pltpu.VMEM((nb, aslot, width), BF16),
        pltpu.VMEM((nb, aslot, 128), jnp.int32),
        pltpu.VMEM((nb * aslot, ntrk), BF16),
    ]
    scratch += [dma((4,)), dma((4,)), dma((nb,)), dma((nb,))] + [dma((nchip,))] * 8 + [dma((2, nb)), dma((2, nb))]
    if spread:
        scratch += [dma, dma((2, nb)), dma((2, nb))] + [dma((2, nb, nchip))] * 4
    args = [x, bn_scale[None], bn_shift[None], mid_scale[None], mid_shift[None]] + weights + [head, targets[0], meta]
    vmem = pl.BlockSpec(memory_space=pltpu.VMEM)
    d_in, new_head = pl.pallas_call(
        functools.partial(kernel, nb, npos, spread),
        out_shape=[
            jax.ShapeDtypeStruct((nrows, width), BF16),
            jax.ShapeDtypeStruct((ntrk, width), BF16),
        ],
        in_specs=[vmem] * len(args),
        out_specs=[vmem] * 2,
        scratch_shapes=scratch,
        compiler_params=pltpu.CompilerParams(
            collective_id=0, has_side_effects=True, vmem_limit_bytes=56 * 1024 * 1024
        ),
        cost_estimate=pl.CostEstimate(flops=7_200_000_000, bytes_accessed=13_000_000, transcendentals=4_000_000),
    )(*args)
    return d_in[None], new_head


def solution(mesh):
    in_specs = (
        P("batch", "pos", None),
        P(),
        P(),
        P(),
        P(),
        P("batch", None, None),
        P("batch", None),
        P("pos", None),
        P("batch", "pos", None),
        P("batch", "pos"),
        P("batch", "pos"),
    )
    out_specs = (P("batch", "pos", None), P("pos", None))
    return jax.shard_map(
        functools.partial(per_device, mesh.shape["batch"], mesh.shape["pos"]),
        mesh=mesh,
        in_specs=in_specs,
        out_specs=out_specs,
        check_vma=False,
    )
```

time: 287 us -> 98.5 us (0.34)
  waiting for transfers between devices: 198 us -> 0 us
  Pallas kernels: 0 us -> 81.5 us
  matrix products: 29 us -> 0 us
  blocking collectives: 17.5 us -> 0 us
  between operations: 15.3 us -> 1.31 us
  other arithmetic: 12.7 us -> 1.79 us
  starting transfers between devices: 8.18 us -> 0 us
  local copies, waits for them, and re-layouts: 5.62 us -> 13.6 us
    all_gather x3 -> x0, waiting for transfers between devices: 93.6 us -> none  [the longest x1 44.9 us: per_device(): lax.all_gather(dilated_weight, 'batch', axis=0, tiled=True)]
    pallas_call x0 -> x1, Pallas kernels: none -> 81.5 us  [per_device(): pl.pallas_call(functools.partial(kernel, nb, npos, spread), out_shape=[ja...]
    psum x1 -> x0, waiting for transfers between devices: 68.3 us -> none  [per_device(): d_head = lax.psum(spread.astype(jnp.bfloat16), 'batch').astype(jnp.float32)]
    reduce_scatter x1 -> x0, waiting for transfers between devices: 34.5 us -> none  [per_device(): lax.psum_scatter(lax.dot_general(delta, embed, (((0,), (0,)), ((), ())),...]
    dot_general x11 -> x0, matrix products: 29 us -> none  [the longest x1 4.33 us: per_device(): lax.dot_general(delta, embed, (((0,), (0,)), ((), ())), preferred_element...]
    unnamed x1 -> x0, blocking collectives: 17.5 us -> none
    convert_element_type x5 -> x0, other arithmetic: 8.4 us -> none  [the longest x1 3.71 us: per_device(): d_head = lax.psum(spread.astype(jnp.bfloat16), 'batch').astype(jnp.float32)]
    ppermute x4 -> x0, starting transfers between devices: 7.98 us -> none  [the longest x2 5.39 us: with_halo(): before = lax.ppermute(last, axis, up)]
  transfers between devices with their start and end apart: 9 -> 0, of which waited for: 5 -> 0; matrix products, arithmetic and copies ran while one was open for 10% -> 0% of each run, Pallas kernels for 0% -> 0%
where the time goes in v1:
time: 98.5 us; the launch traced here: 98.1 us
  Pallas kernels  81.5 us (83%)
  local copies, waits for them, and re-layouts  13.6 us (14%)
  other arithmetic  1.79 us (2%)
  between operations  1.31 us (1%)
    pallas_call x1, Pallas kernels, per_device(): pl.pallas_call(functools.partial(kernel, nb, npos, spread), out_shape=[ja...  81.5 us
    unnamed x5, local copies, waits for them, and re-layouts  6 us

profile of v1, /device:TPU:0, one launch (start us, length us, event | category | flops | bytes accessed | tf_op | source)
XLA Modules:
  0.0 98.1 jit_solution(11469064779449773784)
XLA Ops:
  1.3 0.7 compare_select_fusion
  1.9 1.3 %broadcast_in_dim.27.refs_3_ = f32[1,384]{1,0:T(1,128)} reshape(f32[384]{0:T(512)} %param.14) | data formatting | bytes 3072 | tf_op jit(solution)/shard_map/broadcast_in_dim | solution.py:410
  3.2 1.3 %broadcast_in_dim.28.refs_4_ = f32[1,384]{1,0:T(1,128)} reshape(f32[384]{0:T(512)} %param.15) | data formatting | bytes 3072 | tf_op jit(solution)/shard_map/broadcast_in_dim | solution.py:410
  4.4 1.3 %broadcast_in_dim.25.refs_1_ = f32[1,1536]{1,0:T(1,128)} reshape(f32[1536]{0:T(1024)} %param.12) | data formatting | bytes 12288 | tf_op jit(solution)/shard_map/broadcast_in_dim | solution.py:410
  5.7 1.3 %broadcast_in_dim.26.refs_2_ = f32[1,1536]{1,0:T(1,128)} reshape(f32[1536]{0:T(1024)} %param.13) | data formatting | bytes 12288 | tf_op jit(solution)/shard_map/broadcast_in_dim | solution.py:410
  7.0 0.7 broadcast_in_dim.30.refs_8_
  7.7 1.0 %copy.19 = bf16[12,4,8,384]{3,2,0,1:T(8,128)(2,1)S(1)} copy(bf16[12,4,8,384]{3,2,1,0:T(8,128)(2,1)} %bitcast.16) | data formatting | bytes 589824 | tf_op jit(solution)/shard_map/reshape | solution.py:373
  8.7 1.9 %copy.15 = bf16[384,3,384]{2,1,0:T(4,128)(2,1)S(1)} copy(bf16[384,3,384]{2,0,1:T(8,128)(2,1)} %param.16) | data formatting | bytes 1769472 | tf_op args[5]
  10.7 0.8 concatenate.8
  11.5 1.1 %pad_maximum_fusion.refs_5_ = bf16[8,48,1536]{2,1,0:T(8,128)(2,1)} fusion(bf16[8,48,384]{2,1,0:T(8,128)(2,1)S(1)} %bitcast.15, bf16[8,48,1152]{2,1,0:T(8,128)(2,1)S(1)} %concatenate.8), kind=kLoop, calls=%fused_computation | loop fusion | flops 2359296 | bytes 2359296 | tf_op jit(solution)/shard_map/concatenate | solution.py:374
  12.6 81.5 %shard_map.122 = (bf16[512,1536]{1,0:T(8,128)(2,1)}, bf16[640,1536]{1,0:T(8,128)(2,1)}) custom-call(bf16[512,1536]{1,0:T(8,128)(2,1)} %bitcast.17, f32[1,1536]{1,0:T(1,128)} %broadcast_in_dim.25.refs_1_, f32[1,1536]{1,0:T(1,128)} %broadcast_in_dim.26.refs_2_, f32[1,384]{1,0:T(1,128)} %broadcast_in_dim.27.refs_3_, f32[1,384]{1,0:T(1,128)} %broadcast_in_dim.28.refs_4_, ...), custom_call_target="tpu_custom_call" | custom-call | flops 7200000000 | bytes 13000000 | tf_op jit(solution)/shard_map/pallas_call | solution.py:412
  94.1 0.0 copy-start
  94.1 2.8 %copy.23 = bf16[1,512,1536]{2,1,0:T(8,128)(2,1)} copy(bf16[1,512,1536]{2,1,0:T(8,128)(2,1)} %bitcast.14) | data formatting | bytes 3145728
  96.9 0.0 copy-done
  96.9 1.3 %copy.24 = bf16[640,1536]{1,0:T(8,128)(2,1)} copy(bf16[640,1536]{1,0:T(8,128)(2,1)S(1)} %copy-done) | data formatting | bytes 3932160
Async XLA Ops:
  94.1 2.8 %copy-start = (bf16[640,1536]{1,0:T(8,128)(2,1)S(1)}, bf16[640,1536]{1,0:T(8,128)(2,1)}, u32[]{:S(2)}) copy-start(bf16[640,1536]{1,0:T(8,128)(2,1)} %get-tuple-element.9) | copy-start | bytes 5898244

commit v2 on v1

--- a/solution.py
+++ b/solution.py
@@ -40,20 +40,20 @@
 def kernel(nb, npos, spread, *refs):
     refs = list(refs)
     take = lambda n: [refs.pop(0) for _ in range(n)]
-    x, bsc, bsh, msc, msh, packed = take(6)
-    if not spread:
-        (wp,) = take(1)
-    head, goal, meta = take(3)
+    x_hbm, bsc1, bsh1, msc1, msh1, flat, wpt, head_hbm, goal_hbm, slots, counts = take(11)
     d_in, new_head = take(2)
     if spread:
         w, wp = take(2)
     else:
-        w = packed
+        w, wp = flat, wpt
+    x, head, goal, meta, bsc, bsh, msc, msh, in_sem = take(9)
     acted, hidden, mid, embed, sel, delta, back, dpad, xh = take(9)
     grads, r1buf, part, r2buf, rows_all, meta_all, onehot = take(7)
     (halo_s, halo_r, meta_s, meta_r, sel_s, sel_r, self_s, self_r, r1_s, r1_r, r2_s, r2_r, r3_s, r3_r) = take(14)
     if spread:
         own_sem, w1_s, w1_r, w2_s, w2_r, wf_s, wf_r = take(7)
+        rest = wpt.shape[2] // mid.shape[1]
+        per = npos // rest
 
     z = lax.axis_index("batch")
     p = lax.axis_index("pos")
@@ -78,6 +78,27 @@
     def from_chip(d):
         return lax.rem(chip - d + nchip, nchip)
 
+    loads = []
+    if spread:
+        hc = mid.shape[1]
+        loads.append(pltpu.make_async_copy(flat, w.at[z, :, :, pl.ds(0, 3 * hc)], own_sem.at[0]))
+        for q in range(rest):
+            src = wpt.at[:, :, pl.ds(q * hc, hc)]
+            dst = w.at[z, pl.ds(q * per, per), :, pl.ds(3 * hc, hc)]
+            loads.append(pltpu.make_async_copy(src, dst, own_sem.at[1 + q]))
+    own = len(loads)
+    loads.append(pltpu.make_async_copy(x_hbm, x, in_sem.at[0]))
+    loads.append(pltpu.make_async_copy(head_hbm, head, in_sem.at[1]))
+    loads.append(pltpu.make_async_copy(goal_hbm, goal, in_sem.at[2]))
+    for c in loads:
+        c.start()
+    for src, dst in ((bsc1, bsc), (bsh1, bsh), (msc1, msc), (msh1, msh)):
+        dst[...] = src[...].reshape(dst.shape)
+    spot = lax.broadcasted_iota(jnp.int32, (aslot, aslot), 1)
+    live = jnp.logical_and(spot == lax.broadcasted_iota(jnp.int32, (aslot, aslot), 0), spot < counts[...])
+    column = jnp.sum(jnp.where(live, slots[...] + 1, 0), axis=1, keepdims=True) - 1
+    meta[...] = jnp.broadcast_to(column, meta.shape)
+
     bar = pltpu.get_barrier_semaphore()
     for d in range(1, npos):
         pl.semaphore_signal(bar, inc=1, device_id=(z, lax.rem(p + d, npos)), device_id_type=MESH)
@@ -134,16 +155,22 @@
         return start, arrive, finish
 
     if spread:
-        w_start, w_arrive, w_finish = chain(packed.at[p], lambda zz: w.at[zz, p], w1_s, w1_r)
+        gx, gy = lax.rem(chip, 2), chip // 2
+        xn, yn = (gy * 2 + 1 - gx) * 2 + core, ((1 - gy) * 2 + gx) * 2 + core
+        mine = lax.rem(gx + gy, 2) * 4
+        other = 4 - mine
+        pair = lambda zz, c: w.at[zz, pl.ds(mine + 2 * c, 2)]
+        w_start, w_arrive, w_finish = chain(pair(z, core), lambda zz: pair(zz, core), w1_s, w1_r)
+        for c in loads[:own]:
+            c.wait()
         w_start(0, 0)
         w_start(1, 0)
+    loads[own].wait()
     go(rc(x.at[pl.ds(0, STEP)], xh.at[1], halo_s.at[0], halo_r.at[1], z, left))
     go(rc(x.at[pl.ds(nrows - STEP, STEP)], xh.at[0], halo_s.at[1], halo_r.at[0], z, right))
     for d in range(1, nb):
         go(rc(meta, meta_all.at[z], meta_s.at[d], meta_r.at[d], lax.rem(z + d, nb), p))
-    if spread:
-        own = pltpu.make_async_copy(packed, w.at[z], own_sem)
-        own.start()
+    loads[own + 1].wait()
 
     ntrk = head.shape[0]
 
@@ -162,9 +189,10 @@
 
     def w_spread(di, k):
         def body(zz):
-            for d in range(1, nchip):
-                rc(w.at[zz, p], w.at[zz, p], w2_s.at[di, k, d], w2_r.at[di, k, d], z, at_chip(d) * 2 + core).start()
-            rc(w.at[zz, p], w.at[zz, p], wf_s.at[di, k, 0], wf_r.at[di, k, 0], z, sib).start()
+            for i, to in enumerate((xn, yn)):
+                one = w.at[zz, mine + 2 * core + i]
+                rc(one, one, w2_s.at[di, k, i], w2_r.at[di, k, i], z, to).start()
+            rc(pair(zz, core), pair(zz, core), wf_s.at[di, k, 2], wf_r.at[di, k, 2], z, sib).start()
 
         w_arrive(di, k, body)
 
@@ -178,19 +206,20 @@
 
         @pl.when(has)
         def _():
-            for d in range(1, nchip):
-                q = from_chip(d) * 2 + core
-                rc(w.at[zz, q], w.at[zz, q], w2_s.at[di, k, d], w2_r.at[di, k, d], z, sib).wait_recv()
-                rc(w.at[zz, q], w.at[zz, q], wf_s.at[di, k, d], wf_r.at[di, k, d], z, sib).start()
+            for i in range(2):
+                one = w.at[zz, other + 2 * core + i]
+                rc(one, one, w2_s.at[di, k, i], w2_r.at[di, k, i], z, sib).wait_recv()
+                rc(one, one, wf_s.at[di, k, i], wf_r.at[di, k, i], z, sib).start()
 
     def w_ready(di, k):
         zz, has = w_shard(di, k)
 
         @pl.when(has)
         def _():
-            for d in range(nchip):
-                q = from_chip(d) * 2 + 1 - core
-                rc(w.at[zz, q], w.at[zz, q], wf_s.at[di, k, d], wf_r.at[di, k, d], z, sib).wait_recv()
+            rc(pair(zz, 1 - core), pair(zz, 1 - core), wf_s.at[di, k, 2], wf_r.at[di, k, 2], z, sib).wait_recv()
+            for i in range(2):
+                one = w.at[zz, other + 2 * (1 - core) + i]
+                rc(one, one, wf_s.at[di, k, i], wf_r.at[di, k, i], z, sib).wait_recv()
             conv(zz)
 
     def w_done(di, k):
@@ -198,10 +227,12 @@
 
         @pl.when(has)
         def _():
-            for d in range(1, nchip):
-                rc(w.at[zz, p], w.at[zz, p], w2_s.at[di, k, d], w2_r.at[di, k, d], z, sib).wait_send()
-            for d in range(nchip):
-                rc(w.at[zz, p], w.at[zz, p], wf_s.at[di, k, d], wf_r.at[di, k, d], z, sib).wait_send()
+            for i in range(2):
+                one = w.at[zz, mine + 2 * core + i]
+                rc(one, one, w2_s.at[di, k, i], w2_r.at[di, k, i], z, sib).wait_send()
+                one = w.at[zz, other + 2 * core + i]
+                rc(one, one, wf_s.at[di, k, i], wf_r.at[di, k, i], z, sib).wait_send()
+            rc(pair(zz, core), pair(zz, core), wf_s.at[di, k, 2], wf_r.at[di, k, 2], z, sib).wait_send()
 
     def wrows(zz, lo, n):
         return w[zz, :, :, lo : lo + n].reshape(cw, n)
@@ -226,11 +257,11 @@
             for k in steps[:1]:
                 w_spread(0, k)
                 w_spread(1, k)
-        if i == 1:
+        if i == 2:
             sel_forward()
-            for k in steps[1:2]:
-                w_spread(0, k)
-                w_spread(1, k)
+            for k in steps[:1]:
+                w_forward(0, k)
+                w_forward(1, k)
     for side, edge in ((0, 0), (1, npos - 1)):
         rc(xh.at[side], xh.at[side], halo_s.at[side], halo_r.at[side], z, sib).wait_recv()
         keep = jnp.where(p == edge, 0.0, 1.0)
@@ -240,21 +271,17 @@
             lo = 0 if side == 0 else STEP + nrows
             acted[i, lo : lo + STEP] = (gelu(first) * keep).astype(BF16)
     if spread:
-        for k in steps[2:]:
-            w_forward(0, k - 2)
-            w_forward(1, k - 2)
+        conv(z)
+        for k in steps[1:]:
             w_spread(0, k)
             w_spread(1, k)
-        own.wait()
-        conv(z)
-        for k in steps[max(0, len(steps) - 2) :]:
+            w_ready(0, k - 1)
+            w_ready(1, k - 1)
             w_forward(0, k)
             w_forward(1, k)
-        for k in steps:
+        for k in steps[-1:]:
             w_ready(0, k)
             w_ready(1, k)
-        rest = width // hid
-        per = npos // rest
         for zz in range(nb):
             for q in range(rest):
                 blk = w[zz, q * per : (q + 1) * per, :, 3 * hid : 4 * hid].reshape(cw // rest, hid)
@@ -273,6 +300,7 @@
         q = from_chip(d) * 2 + 1 - core
         rc(sel.at[q], sel.at[q], self_s.at[d], self_r.at[d], z, sib).wait_recv()
 
+    loads[own + 2].wait()
     group = 256
     per_group = group // aslot
     for j in range(0, nslot, group):
@@ -364,19 +392,14 @@
     aslot = assay_slots.shape[1]
     nslot = targets.shape[2]
     ntrk = head.shape[0]
-    spread = cw % (16 * npos) == 0 and cw % 128 == 0 and npos % (width // hid) == 0
+    rest = width // hid
+    spread = npos == 8 and cw % (16 * npos) == 0 and cw % 128 == 0 and npos % rest == 0
     flat = dilated_weight.reshape(cw, 3 * hid)
-    slots = jnp.where(jnp.arange(aslot) < assay_counts[0, 0], assay_slots[0], -1)
-    meta = jnp.broadcast_to(slots[:, None], (aslot, 128))
-    if spread:
-        rest = width // hid
-        wide = jnp.swapaxes(w_point.reshape(w_point.shape[0], rest, hid), 0, 1).reshape(cw, hid)
-        weights = [jnp.concatenate([flat, wide], axis=1).reshape(npos, cw // npos, 4 * hid)]
+    if spread:
+        slab = cw // npos
+        weights = [flat.reshape(npos, slab, 3 * hid), w_point.reshape(npos // rest, slab, width)]
         nz = nb
-        weight_scratch = [
-            pltpu.VMEM((nb, npos, cw // npos, 4 * hid), BF16),
-            pltpu.VMEM((hid, width), BF16),
-        ]
+        weight_scratch = [pltpu.VMEM((nb, npos, slab, 4 * hid), BF16), pltpu.VMEM((hid, width), BF16)]
     else:
         nz = 4
         weights = [
@@ -387,6 +410,15 @@
     nchip = npos // 2
     dma = pltpu.SemaphoreType.DMA
     scratch = weight_scratch + [
+        pltpu.VMEM((nrows, width), BF16),
+        pltpu.VMEM((ntrk, width), BF16),
+        pltpu.VMEM((nrows, nslot), BF16),
+        pltpu.VMEM((aslot, 128), jnp.int32),
+        pltpu.VMEM((1, width), F32),
+        pltpu.VMEM((1, width), F32),
+        pltpu.VMEM((1, hid), F32),
+        pltpu.VMEM((1, hid), F32),
+        dma((3,)),
         pltpu.VMEM((nz, nrows + 2 * STEP, width // nz), BF16),
         pltpu.VMEM((nrows, hid), F32),
         pltpu.VMEM((nrows, hid), BF16),
@@ -406,16 +438,17 @@
     ]
     scratch += [dma((4,)), dma((4,)), dma((nb,)), dma((nb,))] + [dma((nchip,))] * 8 + [dma((2, nb)), dma((2, nb))]
     if spread:
-        scratch += [dma, dma((2, nb)), dma((2, nb))] + [dma((2, nb, nchip))] * 4
-    args = [x, bn_scale[None], bn_shift[None], mid_scale[None], mid_shift[None]] + weights + [head, targets[0], meta]
+        scratch += [dma((1 + rest,)), dma((2, nb)), dma((2, nb))] + [dma((2, nb, 2))] * 2 + [dma((2, nb, 3))] * 2
+    args = [x, bn_scale, bn_shift, mid_scale, mid_shift] + weights + [head, targets[0], assay_slots, assay_counts]
     vmem = pl.BlockSpec(memory_space=pltpu.VMEM)
+    far = pl.BlockSpec(memory_space=pl.ANY)
     d_in, new_head = pl.pallas_call(
         functools.partial(kernel, nb, npos, spread),
         out_shape=[
             jax.ShapeDtypeStruct((nrows, width), BF16),
             jax.ShapeDtypeStruct((ntrk, width), BF16),
         ],
-        in_specs=[vmem] * len(args),
+        in_specs=[far] + [vmem] * 4 + ([far] * 2 if spread else [vmem] * 2) + [far] * 2 + [vmem] * 2,
         out_specs=[vmem] * 2,
         scratch_shapes=scratch,
         compiler_params=pltpu.CompilerParams(

time: 98.5 us -> 87.4 us (0.89)
  local copies, waits for them, and re-layouts: 13.6 us -> 7.95 us
  Pallas kernels: 81.5 us -> 78 us
  other arithmetic: 1.79 us -> 0 us
    broadcast_in_dim x5 -> x0, local copies, waits for them, and re-layouts: 5.79 us -> none  [the longest x1 1.3 us: per_device(): bn_scale[None]]
    pallas_call x1, Pallas kernels: 81.5 us -> 78 us  [per_device(): pl.pallas_call(functools.partial(kernel, nb, npos, spread), out_shape=[ja...]
    another operation x0 -> x1, local copies, waits for them, and re-layouts: none -> 1.95 us  [per_device(): flat.reshape(npos, slab, 3 * hid)]
    concatenate x1 -> x0, other arithmetic: 1.13 us -> none  [per_device(): jnp.concatenate([flat, wide], axis=1).reshape(npos, cw // npos, 4 * hid)]
    reshape x1 -> x0, local copies, waits for them, and re-layouts: 0.99 us -> none  [per_device(): w_point.reshape(w_point.shape[0], rest, hid)]
where the time goes in v2:
time: 87.4 us; the launch traced here: 87.2 us
  Pallas kernels  78 us (89%)
  local copies, waits for them, and re-layouts  7.95 us (9%)
  between operations  1.3 us (1%)
    pallas_call x1, Pallas kernels, per_device(): pl.pallas_call(functools.partial(kernel, nb, npos, spread), out_shape=[ja...  78 us
    unnamed x5, local copies, waits for them, and re-layouts  6 us
    another operation x1, local copies, waits for them, and re-layouts, per_device(): flat.reshape(npos, slab, 3 * hid)  1.95 us

profile of v2, /device:TPU:0, one launch (start us, length us, event | category | flops | bytes accessed | tf_op | source)
XLA Modules:
  0.0 87.2 jit_solution(7381684743023368105)
XLA Ops:
  1.3 1.9 %copy.14 = bf16[384,3,384]{2,1,0:T(4,128)(2,1)S(1)} copy(bf16[384,3,384]{2,0,1:T(8,128)(2,1)} %param.16) | data formatting | bytes 1769472 | tf_op args[5]
  3.2 2.0 %reshape_reshape.3.refs_5_ = bf16[8,48,1152]{2,1,0:T(8,128)(2,1)} reshape(bf16[384,3,384]{2,1,0:T(4,128)(2,1)S(1)} %copy.14) | data formatting | bytes 1769472 | tf_op jit(solution)/shard_map/reshape;reshape | solution.py:400
  5.2 78.0 %shard_map.122 = (bf16[512,1536]{1,0:T(8,128)(2,1)}, bf16[640,1536]{1,0:T(8,128)(2,1)}) custom-call(bf16[512,1536]{1,0:T(8,128)(2,1)} %bitcast.5, f32[1536]{0:T(1024)} %refs_1_.1, f32[1536]{0:T(1024)} %refs_2_.1, f32[384]{0:T(512)} %refs_3_.1, f32[384]{0:T(512)} %refs_4_.1, bf16[8,48,1152]{2,1,0:T(8,128)(2,1)} %reshape_reshape.3.refs_5_, ...), custom_call_target="tpu_custom_call" | custom-call | flops 7200000000 | bytes 13000000 | tf_op jit(solution)/shard_map/pallas_call | solution.py:445
  83.1 0.0 copy-start
  83.2 2.8 %copy.18 = bf16[1,512,1536]{2,1,0:T(8,128)(2,1)} copy(bf16[1,512,1536]{2,1,0:T(8,128)(2,1)} %bitcast.4) | data formatting | bytes 3145728
  85.9 0.0 copy-done
  85.9 1.3 %copy.19 = bf16[640,1536]{1,0:T(8,128)(2,1)} copy(bf16[640,1536]{1,0:T(8,128)(2,1)S(1)} %copy-done) | data formatting | bytes 3932160
Async XLA Ops:
  83.1 2.8 %copy-start = (bf16[640,1536]{1,0:T(8,128)(2,1)S(1)}, bf16[640,1536]{1,0:T(8,128)(2,1)}, u32[]{:S(2)}) copy-start(bf16[640,1536]{1,0:T(8,128)(2,1)} %get-tuple-element.9) | copy-start | bytes 5898244

commit v3 on v2

--- a/solution.py
+++ b/solution.py
@@ -81,11 +81,12 @@
     loads = []
     if spread:
         hc = mid.shape[1]
-        loads.append(pltpu.make_async_copy(flat, w.at[z, :, :, pl.ds(0, 3 * hc)], own_sem.at[0]))
+        for k in range(3):
+            loads.append(pltpu.make_async_copy(flat.at[k], w.at[z, :, :, pl.ds(k * hc, hc)], own_sem.at[rest + k]))
         for q in range(rest):
             src = wpt.at[:, :, pl.ds(q * hc, hc)]
             dst = w.at[z, pl.ds(q * per, per), :, pl.ds(3 * hc, hc)]
-            loads.append(pltpu.make_async_copy(src, dst, own_sem.at[1 + q]))
+            loads.append(pltpu.make_async_copy(src, dst, own_sem.at[q]))
     own = len(loads)
     loads.append(pltpu.make_async_copy(x_hbm, x, in_sem.at[0]))
     loads.append(pltpu.make_async_copy(head_hbm, head, in_sem.at[1]))
@@ -397,7 +398,7 @@
     flat = dilated_weight.reshape(cw, 3 * hid)
     if spread:
         slab = cw // npos
-        weights = [flat.reshape(npos, slab, 3 * hid), w_point.reshape(npos // rest, slab, width)]
+        weights = [jnp.swapaxes(dilated_weight, 0, 1).reshape(3, npos, slab, hid), w_point.reshape(npos // rest, slab, width)]
         nz = nb
         weight_scratch = [pltpu.VMEM((nb, npos, slab, 4 * hid), BF16), pltpu.VMEM((hid, width), BF16)]
     else:
@@ -438,7 +439,7 @@
     ]
     scratch += [dma((4,)), dma((4,)), dma((nb,)), dma((nb,))] + [dma((nchip,))] * 8 + [dma((2, nb)), dma((2, nb))]
     if spread:
-        scratch += [dma((1 + rest,)), dma((2, nb)), dma((2, nb))] + [dma((2, nb, 2))] * 2 + [dma((2, nb, 3))] * 2
+        scratch += [dma((3 + rest,)), dma((2, nb)), dma((2, nb))] + [dma((2, nb, 2))] * 2 + [dma((2, nb, 3))] * 2
     args = [x, bn_scale, bn_shift, mid_scale, mid_shift] + weights + [head, targets[0], assay_slots, assay_counts]
     vmem = pl.BlockSpec(memory_space=pltpu.VMEM)
     far = pl.BlockSpec(memory_space=pl.ANY)

time: 87.4 us -> 83.6 us (0.957)
  local copies, waits for them, and re-layouts: 7.95 us -> 4.07 us
    another operation x1 -> x0, local copies, waits for them, and re-layouts: 1.95 us -> none  [per_device(): flat.reshape(npos, slab, 3 * hid)]
    unnamed x5 -> x4, local copies, waits for them, and re-layouts: 6 us -> 4.07 us
where the time goes in v3:
time: 83.6 us; the launch traced here: 83.4 us
  Pallas kernels  78 us (93%)
  local copies, waits for them, and re-layouts  4.07 us (5%)
  between operations  1.3 us (2%)
    pallas_call x1, Pallas kernels, per_device(): pl.pallas_call(functools.partial(kernel, nb, npos, spread), out_shape=[ja...  78 us
    unnamed x4, local copies, waits for them, and re-layouts  4.07 us

profile of v3, /device:TPU:0, one launch (start us, length us, event | category | flops | bytes accessed | tf_op | source)
XLA Modules:
  0.0 83.4 jit_solution(10312876230680427328)
XLA Ops:
  1.3 78.0 %shard_map.122 = (bf16[512,1536]{1,0:T(8,128)(2,1)}, bf16[640,1536]{1,0:T(8,128)(2,1)}) custom-call(bf16[512,1536]{1,0:T(8,128)(2,1)} %bitcast.8, f32[1536]{0:T(1024)} %refs_1_.1, f32[1536]{0:T(1024)} %refs_2_.1, f32[384]{0:T(512)} %refs_3_.1, f32[384]{0:T(512)} %refs_4_.1, bf16[3,8,48,384]{3,2,1,0:T(8,128)(2,1)} %bitcast.9, bf16[2,48,1536]{2,1,0:T(8,128)(2,1)} %bitcast.11, ...), custom_call_target="tpu_custom_call" | custom-call | flops 7200000000 | bytes 13000000 | tf_op jit(solution)/shard_map/pallas_call | solution.py:446
  79.3 0.0 copy-start
  79.3 2.8 %copy.16 = bf16[1,512,1536]{2,1,0:T(8,128)(2,1)} copy(bf16[1,512,1536]{2,1,0:T(8,128)(2,1)} %bitcast.7) | data formatting | bytes 3145728
  82.1 0.0 copy-done
  82.1 1.3 %copy.17 = bf16[640,1536]{1,0:T(8,128)(2,1)} copy(bf16[640,1536]{1,0:T(8,128)(2,1)S(1)} %copy-done) | data formatting | bytes 3932160
Async XLA Ops:
  79.3 2.8 %copy-start = (bf16[640,1536]{1,0:T(8,128)(2,1)S(1)}, bf16[640,1536]{1,0:T(8,128)(2,1)}, u32[]{:S(2)}) copy-start(bf16[640,1536]{1,0:T(8,128)(2,1)} %get-tuple-element.9) | copy-start | bytes 5898244
